TPU v7x, 32 devices: a whole 2x2x4 slice. The times are simulated.
32 devices in a mesh: groups: 2 (over y), mem: 8 (over z, x), lat: 2 (over core).
Axes of the slice: x: 2, y: 2, z: 4, core: 2. Of those that a mesh axis runs over, the one named last changes fastest.
Arguments:
- state: bfloat16 [64, 8, 64, 512], P(('groups', 'mem'), None, 'lat'), parts along dimension 0, may hold values from -6 to 6
- counts: int32 [16], P(('groups', 'mem')), parts along dimension 0, may hold values from 1 to 4, 16 in all
- east_wind: float32 [128, 512], P(('groups', 'lat')), parts along dimension 0, may hold values from -0.48 to 0.48
- north_wind: float32 [128, 512], P(('groups', 'lat')), parts along dimension 0, may hold values from -0.48 to 0.48
- obs_cells: int32 [4, 32768], P(('groups', 'lat')), parts along dimension 0, may hold values from 0 to 16383
- obs_mask: int32 [4, 32768], P(('groups', 'lat')), parts along dimension 0, may hold values 0 or 1
- obs_values: float32 [4, 32768], P(('groups', 'lat')), parts along dimension 0, may hold values from -6 to 6
- obs_error: float32 [4, 32768], P(('groups', 'lat')), parts along dimension 0, may hold values from 0.2 to 2
- relax: float32 [8], replicated, may hold values from 0.3 to 0.9
Outputs:
- new_state: bfloat16 [64, 8, 64, 512], P(('groups', 'mem'), None, 'lat'), parts along dimension 0
- analysis_mean: bfloat16 [16, 64, 512], P('groups', 'lat'), parts along dimension 0
There are 2 independent parts, one for each index of `groups`. A program takes and returns all parts, laid end to end along the dimension named above; an argument that names none is the same for every part. Nothing has to cross between parts.
Inputs may be any that keep to these rules, and one draw needn't show every extreme that they name: counts over the mem axis add up to 16, and some mem index holds 4 members.
All inputs are finite; a program needn't handle non-finite values. No bound on the sum of `counts` or of `obs_mask` on one device may be relied on, other than what follows from the above.
Results may differ from a plain program's by a relative error of at most 0.001.
The roundings to bfloat16 on the way count: a program that leaves them out, or rounds other values in their place, can miss the bound.
Values may be sent and summed in bfloat16 or wider, within the bound.
A program may use at most 128 MiB of HBM per device.

v0:
```python
import functools

import jax
import jax.numpy as jnp
from jax import lax
from jax.experimental import pallas as pl
from jax.experimental.pallas import tpu as pltpu
from jax.sharding import PartitionSpec as P

STEPS = 4
SMOOTH = 16
LOG_TWO_PI = 1.8378770664093453
MESH = pl.DeviceIdType.MESH
TILE_ROWS = 16
TILE_COLS = 128
OBS_BLOCK = 2048


def pieces(values):
    high = values.astype(jnp.bfloat16).astype(jnp.float32)
    rest = values - high
    mid = rest.astype(jnp.bfloat16).astype(jnp.float32)
    return high, mid, rest - mid


def partial_grids(rows, width, cells, mask, values, error):
    count = cells.shape[1]
    used = mask.astype(jnp.float32)
    inverse = used / (error * error)
    terms = (
        inverse,
        inverse * values,
        inverse * values * values + used * (2.0 * jnp.log(error) + LOG_TWO_PI),
    )
    row = cells // width
    column = cells - row * width
    row_hit = lax.broadcasted_iota(jnp.int32, (rows, count), 0) == row
    column_hit = jnp.where(
        lax.broadcasted_iota(jnp.int32, (width, count), 0) == column, 1.0, 0.0
    ).astype(jnp.bfloat16)
    left = jnp.concatenate(
        [
            jnp.where(row_hit, piece, 0.0).astype(jnp.bfloat16)
            for term in terms
            for piece in pieces(term)
        ],
        axis=0,
    )
    return lax.dot_general(
        left, column_hit, (((1,), (1,)), ((), ())), preferred_element_type=jnp.float32
    )


def kernel_values(offset):
    values = jnp.exp(-((2.0 * offset.astype(jnp.float32) / SMOOTH) ** 2))
    return jnp.where(jnp.abs(offset) <= SMOOTH, values, 0.0)


def cycle_kernel(
    n,
    state_ref,
    counts_ref,
    east_ref,
    north_ref,
    cells_ref,
    mask_ref,
    values_ref,
    error_ref,
    relax_ref,
    out_ref,
    mean_ref,
    cells,
    mask,
    values,
    error,
    state,
    counted,
    obs_send,
    obs_recv,
    grids,
    halo,
    wind_in,
    wind_halo,
    winds,
    advected,
    lon_kernel,
    loglik,
    loglik_halo,
    scores,
    send,
    recv,
    pair,
    merged,
    halo_sems,
    send_sems,
    recv_sems,
    back_send,
    back_recv,
    relay_send,
    local_sems,
    obs_sems,
    obs_arrived,
    grid_sems,
    grid_arrived,
):
    slots, fields, rows, width = state_ref.shape
    across = width // TILE_COLS
    owners = (rows // TILE_ROWS) * across
    me = lax.axis_index("mem")
    band = lax.axis_index("lat")
    other = 1 - band

    share = cells.shape[1]
    mine = pl.ds(pl.multiple_of(me * share, 128), share)
    loads = [
        pltpu.make_async_copy(source, target, local_sems.at[k])
        for k, (source, target) in enumerate(
            (
                (cells_ref.at[:, mine], cells),
                (mask_ref.at[:, mine], mask),
                (values_ref.at[:, mine], values),
                (error_ref.at[:, mine], error),
                (state_ref, state),
            )
        )
    ]
    for load in loads:
        load.start()

    barrier = pltpu.get_barrier_semaphore()

    def greet(d, carry):
        pl.semaphore_signal(
            barrier, inc=1, device_id={"mem": lax.rem(me + d, n)}, device_id_type=MESH
        )
        return carry

    pl.semaphore_signal(barrier, inc=1, device_id={"lat": other}, device_id_type=MESH)
    lax.fori_loop(1, n, greet, 0)

    wind_in[0] = east_ref[...]
    wind_in[1] = north_ref[...]
    i0 = lax.broadcasted_iota(jnp.int32, (width, width), 0)
    i1 = lax.broadcasted_iota(jnp.int32, (width, width), 1)
    apart = jnp.abs(i0 - i1)
    lon_kernel[...] = kernel_values(jnp.minimum(apart, width - apart))

    pl.semaphore_wait(barrier, n)

    def to_other(source, target, slot):
        copy = pltpu.make_async_remote_copy(
            src_ref=source,
            dst_ref=target,
            send_sem=halo_sems.at[0, slot],
            recv_sem=halo_sems.at[1, slot],
            device_id={"lat": other},
            device_id_type=MESH,
        )
        copy.start()
        return copy

    edge16 = pl.ds(pl.multiple_of(other * (rows - 16), 16), 16)
    edge8 = pl.ds(pl.multiple_of(other * (rows - 8), 8), 8)
    copy_winds = to_other(wind_in.at[:, edge8, :], wind_halo, 0)
    copy_state = to_other(state_ref.at[:, :, edge16, :], halo, 1)

    def tile(t):
        down = t // across
        return (
            pl.ds(pl.multiple_of(down * TILE_ROWS, TILE_ROWS), TILE_ROWS),
            pl.ds(pl.multiple_of((t - down * across) * TILE_COLS, TILE_COLS), TILE_COLS),
        )

    for load in loads[:4]:
        load.wait()
    block = min(share, OBS_BLOCK)
    for start in range(0, share, block):
        part = partial_grids(
            rows, width, *(ref[:, start : start + block] for ref in (cells, mask, values, error))
        )
        for term in range(3):
            base = 3 * term * rows
            terms = (
                part[base : base + rows]
                + part[base + rows : base + 2 * rows]
                + part[base + 2 * rows : base + 3 * rows]
            )
            if start == 0:
                counted[term] = terms
            else:
                counted[term] += terms

    def obs_out(t):
        return pltpu.make_async_remote_copy(
            src_ref=obs_send.at[t],
            dst_ref=obs_recv.at[me],
            send_sem=obs_sems.at[t],
            recv_sem=obs_arrived.at[me],
            device_id={"mem": t},
            device_id_type=MESH,
        )

    def give(j, carry):
        t = lax.rem(me + 1 + j, owners)
        down, along = tile(t)
        for term in range(3):
            obs_send[t, term] = counted[term, down, along]

        @pl.when(t != me)
        def _():
            obs_out(t).start()

        return carry

    lax.fori_loop(0, owners, give, 0)

    def grid_out(d):
        return pltpu.make_async_remote_copy(
            src_ref=grids.at[me],
            dst_ref=grids.at[me],
            send_sem=grid_sems.at[d],
            recv_sem=grid_arrived.at[me],
            device_id={"mem": lax.rem(me + d, n)},
            device_id_type=MESH,
        )

    near = lax.broadcasted_iota(jnp.int32, (8, width), 0)
    keep = jnp.where(band == 0, near, 7 - near) < STEPS

    copy_winds.wait()
    for kind in range(2):
        own = wind_in[kind]
        far = jnp.where(keep, wind_halo[kind], 0.0)
        whole = jnp.concatenate([own, far], axis=0)
        winds[2 * kind] = jnp.abs(whole)
        winds[2 * kind + 1] = whole
    loads[4].wait()
    copy_state.wait()

    def move(index, carry):
        kind = index // slots
        slot = lax.rem(index, slots)
        own = state[slot, kind].astype(jnp.float32)
        far = halo[slot, kind].astype(jnp.float32)
        far = jnp.where(band == 0, far[:8], far[8:])
        far = jnp.where(keep, far, 0.0)
        x = jnp.concatenate([own, far], axis=0)
        for _ in range(STEPS):
            west = pltpu.roll(x, 1, 1)
            east = pltpu.roll(x, width - 1, 1)
            south = pltpu.roll(x, 1, 0)
            north = pltpu.roll(x, rows + 7, 0)
            x = (
                x
                - winds[0] * (x - jnp.where(winds[1] > 0.0, west, east))
                - winds[2] * (x - jnp.where(winds[3] > 0.0, south, north))
            )
        advected[slot, kind] = x[:rows].astype(jnp.bfloat16)
        return carry

    total = slots * fields
    early, late = 3 * total // 8, 6 * total // 8
    lax.fori_loop(0, early, move, 0)

    @pl.when(me < owners)
    def _():
        def arrive(d, carry):
            source = lax.rem(me + n - d, n)
            pltpu.make_async_remote_copy(
                src_ref=obs_send.at[0],
                dst_ref=obs_recv.at[source],
                send_sem=obs_sems.at[0],
                recv_sem=obs_arrived.at[source],
                device_id={"mem": source},
                device_id_type=MESH,
            ).wait_recv()
            return carry

        lax.fori_loop(1, n, arrive, 0)
        obs_recv[me] = obs_send[me]
        grids[me] = lax.fori_loop(1, n, lambda d, sums: sums + obs_recv[d], obs_recv[0])

        def start(d, carry):
            grid_out(d).start()
            return carry

        lax.fori_loop(1, n, start, 0)

    lax.fori_loop(early, late, move, 0)

    def likely(t, carry):
        @pl.when(t != me)
        def _():
            pltpu.make_async_remote_copy(
                src_ref=grids.at[t],
                dst_ref=grids.at[t],
                send_sem=grid_sems.at[0],
                recv_sem=grid_arrived.at[t],
                device_id={"mem": t},
                device_id_type=MESH,
            ).wait_recv()

        down, along = tile(t)
        for slot in range(slots):
            value = advected[slot, 0, down, along].astype(jnp.float32)
            loglik[slot, down, along] = -0.5 * (
                grids[t, 0] * value * value - 2.0 * grids[t, 1] * value + grids[t, 2]
            )
        return carry

    lax.fori_loop(0, owners, likely, 0)
    copy_loglik = to_other(loglik.at[:, edge16, :], loglik_halo, 2)
    lax.fori_loop(late, total, move, 0)

    r0 = lax.broadcasted_iota(jnp.int32, (rows, rows), 0)
    r1 = lax.broadcasted_iota(jnp.int32, (rows, rows), 1)
    own_band = kernel_values(r0 - r1)
    h0 = lax.broadcasted_iota(jnp.int32, (rows, 16), 0)
    h1 = lax.broadcasted_iota(jnp.int32, (rows, 16), 1)
    far_band = kernel_values(jnp.where(band == 0, rows + h1 - h0, h0 + 16 - h1))
    dot = functools.partial(
        jnp.dot, precision=lax.Precision.HIGHEST, preferred_element_type=jnp.float32
    )
    copy_loglik.wait()
    smoothed = jnp.concatenate(
        [
            dot(own_band, loglik[slot]) + dot(far_band, loglik_halo[slot])
            for slot in range(slots)
        ],
        axis=0,
    )
    scores[...] = dot(smoothed, lon_kernel[...]).reshape(slots, rows, width)

    partner = me + 1 - 2 * lax.rem(me, 2)
    parity = lax.rem(me, 2)

    def outgoing(t):
        return pltpu.make_async_remote_copy(
            src_ref=send.at[t],
            dst_ref=recv.at[me // 2],
            send_sem=send_sems.at[t],
            recv_sem=recv_sems.at[me // 2],
            device_id={"mem": t},
            device_id_type=MESH,
        )

    def across_pair(t):
        return pltpu.make_async_remote_copy(
            src_ref=send.at[t],
            dst_ref=pair.at[t // 2],
            send_sem=send_sems.at[t],
            recv_sem=recv_sems.at[n // 2 + t // 2],
            device_id={"mem": partner},
            device_id_type=MESH,
        )

    def gather(t):
        down, along = tile(t)
        live = [
            jnp.where(slot < counts_ref[0], scores[slot, down, along], -jnp.inf)
            for slot in range(slots)
        ]
        peak = functools.reduce(jnp.maximum, live)
        gains = [jnp.exp(score - peak) for score in live]
        send[t, fields] = functools.reduce(jnp.add, gains)
        send[t, fields + 1] = peak
        for kind in range(fields):
            send[t, kind] = functools.reduce(
                jnp.add,
                [
                    gains[slot] * advected[slot, kind, down, along].astype(jnp.float32)
                    for slot in range(slots)
                ],
            )

    def give_pair(j, carry):
        t = lax.rem(partner + 4 + 2 * j, owners)
        gather(t)
        across_pair(t).start()
        return carry

    def give_owner(j, carry):
        t = lax.rem(me + 4 + 2 * j, owners)
        across_pair(t).wait_recv()
        low = send[t, fields + 1]
        high = pair[t // 2, fields + 1]
        peak = jnp.maximum(low, high)
        low = jnp.exp(low - peak)
        high = jnp.exp(high - peak)
        for kind in range(fields + 1):
            send[t, kind] = low * send[t, kind] + high * pair[t // 2, kind]
        send[t, fields + 1] = peak

        @pl.when(t != me)
        def _():
            outgoing(t).start()

        return carry

    def keep_own(j, carry):
        gather(2 * j + parity)
        return carry

    lax.fori_loop(0, owners // 2, give_pair, 0)
    lax.fori_loop(0, owners // 2, keep_own, 0)
    lax.fori_loop(0, owners // 2, give_owner, 0)

    def back(d):
        return pltpu.make_async_remote_copy(
            src_ref=merged.at[me],
            dst_ref=merged.at[me],
            send_sem=back_send.at[d],
            recv_sem=back_recv.at[me],
            device_id={"mem": lax.rem(me + 2 * d, n)},
            device_id_type=MESH,
        )

    def relay(t):
        return pltpu.make_async_remote_copy(
            src_ref=merged.at[t],
            dst_ref=merged.at[t],
            send_sem=relay_send.at[t],
            recv_sem=back_recv.at[t],
            device_id={"mem": partner},
            device_id_type=MESH,
        )

    @pl.when(me < owners)
    def _():
        def arrive(d, carry):
            source = lax.rem(me + 2 * d, n)
            pltpu.make_async_remote_copy(
                src_ref=send.at[0],
                dst_ref=recv.at[source // 2],
                send_sem=send_sems.at[0],
                recv_sem=recv_sems.at[source // 2],
                device_id={"mem": source},
                device_id_type=MESH,
            ).wait_recv()
            return carry

        lax.fori_loop(1, n // 2, arrive, 0)
        recv[me // 2] = send[me]
        peak = lax.fori_loop(
            1,
            n // 2,
            lambda d, top: jnp.maximum(top, recv[d, fields + 1]),
            recv[0, fields + 1],
        )

        def add(d, sums):
            factor = jnp.exp(recv[d, fields + 1] - peak)
            return tuple(sums[k] + factor * recv[d, k] for k in range(fields + 1))

        zero = jnp.zeros((TILE_ROWS, TILE_COLS), jnp.float32)
        sums = lax.fori_loop(0, n // 2, add, (zero,) * (fields + 1))
        for kind in range(fields):
            merged[me, kind] = sums[kind] / sums[fields]

        def start(d, carry):
            back(d).start()
            return carry

        lax.fori_loop(1, n // 2, start, 0)

    def landed(t):
        @pl.when(t != me)
        def _():
            relay(t).wait_recv()

    def pass_on(j, carry):
        t = lax.rem(me + owners - 2 * j, owners)
        landed(t)
        relay(t).start()
        finish(t)
        return carry

    def accept(j, carry):
        t = lax.rem(partner + owners - 2 * j, owners)
        landed(t)
        finish(t)
        return carry

    def finish(t):
        down, along = tile(t)
        for kind in range(fields):
            mean = merged[t, kind]
            mean_ref[kind, down, along] = mean.astype(jnp.bfloat16)
            for slot in range(slots):
                value = advected[slot, kind, down, along].astype(jnp.float32)
                fresh = value + relax_ref[kind] * (mean - value)
                out_ref[slot, kind, down, along] = jnp.where(
                    slot < counts_ref[0], fresh, 0.0
                ).astype(jnp.bfloat16)

    lax.fori_loop(0, owners // 2, pass_on, 0)
    lax.fori_loop(0, owners // 2, accept, 0)

    def sent(t, carry):
        @pl.when(t != me)
        def _():
            obs_out(t).wait_send()

        return carry

    lax.fori_loop(0, owners, sent, 0)

    def passed(j, carry):
        across_pair(2 * j + 1 - parity).wait_send()

        @pl.when(2 * j + parity != me)
        def _():
            outgoing(2 * j + parity).wait_send()

        relay(2 * j + parity).wait_send()
        return carry

    lax.fori_loop(0, owners // 2, passed, 0)

    @pl.when(me < owners)
    def _():
        def sent_back(d, carry):
            back(d).wait_send()
            return carry

        lax.fori_loop(1, n // 2, sent_back, 0)

        def sent_grids(d, carry):
            grid_out(d).wait_send()
            return carry

        lax.fori_loop(1, n, sent_grids, 0)


def cycle(n, state, counts, east_wind, north_wind, obs, relax):
    slots, fields, rows, width = state.shape
    owners = (rows // TILE_ROWS) * (width // TILE_COLS)
    share = obs[0].shape[1] // n
    tile = (TILE_ROWS, TILE_COLS)
    hbm = pl.BlockSpec(memory_space=pl.ANY)
    vmem = pl.BlockSpec(memory_space=pltpu.VMEM)
    smem = pl.BlockSpec(memory_space=pltpu.SMEM)
    f32, bf16 = jnp.float32, jnp.bfloat16
    return pl.pallas_call(
        functools.partial(cycle_kernel, n),
        out_shape=(
            pltpu.VMEM(state.shape, bf16),
            pltpu.VMEM((fields, rows, width), bf16),
        ),
        in_specs=[hbm, smem, vmem, vmem, hbm, hbm, hbm, hbm, smem],
        out_specs=(vmem, vmem),
        scratch_shapes=[
            pltpu.VMEM((1, share), jnp.int32),
            pltpu.VMEM((1, share), jnp.int32),
            pltpu.VMEM((1, share), f32),
            pltpu.VMEM((1, share), f32),
            pltpu.VMEM(state.shape, bf16),
            pltpu.VMEM((3, rows, width), f32),
            pltpu.VMEM((owners, 3) + tile, f32),
            pltpu.VMEM((n, 3) + tile, f32),
            pltpu.VMEM((owners, 3) + tile, f32),
            pltpu.VMEM((slots, fields, 16, width), bf16),
            pltpu.VMEM((2, rows, width), f32),
            pltpu.VMEM((2, 8, width), f32),
            pltpu.VMEM((4, rows + 8, width), f32),
            pltpu.VMEM((slots, fields, rows, width), bf16),
            pltpu.VMEM((width, width), f32),
            pltpu.VMEM((slots, rows, width), f32),
            pltpu.VMEM((slots, 16, width), f32),
            pltpu.VMEM((slots, rows, width), f32),
            pltpu.VMEM((owners, fields + 2, TILE_ROWS, TILE_COLS), f32),
            pltpu.VMEM((n // 2, fields + 2, TILE_ROWS, TILE_COLS), f32),
            pltpu.VMEM((owners // 2, fields + 2, TILE_ROWS, TILE_COLS), f32),
            pltpu.VMEM((owners, fields, TILE_ROWS, TILE_COLS), f32),
            pltpu.SemaphoreType.DMA((2, 3)),
            pltpu.SemaphoreType.DMA((owners,)),
            pltpu.SemaphoreType.DMA((n,)),
            pltpu.SemaphoreType.DMA((n,)),
            pltpu.SemaphoreType.DMA((owners,)),
            pltpu.SemaphoreType.DMA((owners,)),
            pltpu.SemaphoreType.DMA((5,)),
            pltpu.SemaphoreType.DMA((owners,)),
            pltpu.SemaphoreType.DMA((n,)),
            pltpu.SemaphoreType.DMA((n,)),
            pltpu.SemaphoreType.DMA((owners,)),
        ],
        compiler_params=pltpu.CompilerParams(
            collective_id=0, has_side_effects=True, vmem_limit_bytes=56 * 1024 * 1024
        ),
    )(state, counts, east_wind, north_wind, *obs, relax)


def write_kernel(fresh, mean, out, mean_out, sems):
    copies = [
        pltpu.make_async_copy(fresh, out, sems.at[0]),
        pltpu.make_async_copy(mean, mean_out, sems.at[1]),
    ]
    for copy in copies:
        copy.start()
    for copy in copies:
        copy.wait()


def write_out(fresh, mean):
    hbm = pl.BlockSpec(memory_space=pl.ANY)
    return pl.pallas_call(
        write_kernel,
        out_shape=(
            jax.ShapeDtypeStruct(fresh.shape, fresh.dtype),
            jax.ShapeDtypeStruct(mean.shape, mean.dtype),
        ),
        in_specs=[hbm, hbm],
        out_specs=(hbm, hbm),
        scratch_shapes=[pltpu.SemaphoreType.DMA((2,))],
    )(*(pltpu.with_memory_space_constraint(x, pltpu.VMEM) for x in (fresh, mean)))


def on_device(
    n, state, counts, east_wind, north_wind, obs_cells, obs_mask, obs_values, obs_error, relax
):
    obs = (obs_cells, obs_mask, obs_values, obs_error)
    fresh, mean = cycle(n, state, counts, east_wind, north_wind, obs, relax)
    return write_out(fresh, mean)


def solution(mesh):
    return jax.shard_map(
        functools.partial(on_device, mesh.shape["mem"]),
        mesh=mesh,
        in_specs=(
            P(("groups", "mem"), None, "lat", None),
            P(("groups", "mem")),
            P(("groups", "lat"), None),
            P(("groups", "lat"), None),
            P(("groups", "lat"), None),
            P(("groups", "lat"), None),
            P(("groups", "lat"), None),
            P(("groups", "lat"), None),
            P(),
        ),
        out_specs=(P(("groups", "mem"), None, "lat", None), P("groups", "lat", None)),
        check_vma=False,
    )
```

profile of v0, /device:TPU:0, one launch (start us, length us, event | category | flops | bytes accessed | tf_op | source)
XLA Modules:
  0.0 49.6 jit_solution(14302135238015565332)
XLA Ops:
  1.3 47.2 %shard_map.104 = (bf16[4,8,32,512]{3,2,1,0:T(8,128)(2,1)S(1)}, bf16[8,32,512]{2,1,0:T(8,128)(2,1)S(1)}) custom-call(bf16[4,8,32,512]{3,2,1,0:T(8,128)(2,1)} %state_ref.1, s32[1]{0:T(128)S(6)} %copy.11.counts_ref, f32[32,512]{1,0:T(8,128)} %east_ref.1, f32[32,512]{1,0:T(8,128)} %north_ref.1, s32[1,32768]{1,0:T(1,128)} %cells_ref.1, s32[1,32768]{1,0:T(1,128)} %mask_ref.1, ...), custom_call_target="tpu_custom_call" | custom-call | tf_op jit(solution)/shard_map/pallas_call | solution.py:544
  48.5 1.1 %shard_map.105 = (bf16[4,8,32,512]{3,2,1,0:T(8,128)(2,1)}, bf16[8,32,512]{2,1,0:T(8,128)(2,1)}) custom-call(bf16[4,8,32,512]{3,2,1,0:T(8,128)(2,1)S(1)} %get-tuple-element.4.fresh, bf16[8,32,512]{2,1,0:T(8,128)(2,1)S(1)} %get-tuple-element.5.mean), custom_call_target="tpu_custom_call" | custom-call | tf_op jit(solution)/shard_map/pallas_call | solution.py:606
where the time goes:
time: 49.8 us; the launch traced here: 49.6 us
  Pallas kernels  48.3 us (97%)
  between operations  1.29 us (3%)
    pallas_call x1, Pallas kernels, cycle(): pl.pallas_call(functools.partial(cycle_kernel, n), out_shape=(pltpu.VMEM(...  47.2 us
    pallas_call x1, Pallas kernels, write_out(): pl.pallas_call(write_kernel, out_shape=(jax.ShapeDtypeStruct(fresh.shape,...  1.07 us

commit v1 on v0

--- a/solution.py
+++ b/solution.py
@@ -1,4 +1,5 @@
 import functools
+import math
 
 import jax
 import jax.numpy as jnp
@@ -14,6 +15,9 @@
 TILE_ROWS = 16
 TILE_COLS = 128
 OBS_BLOCK = 2048
+LEVELS = 32760.0
+OCTAVE = 128.0
+TINY = 1e-33
 
 
 def pieces(values):
@@ -54,6 +58,22 @@
 def kernel_values(offset):
     values = jnp.exp(-((2.0 * offset.astype(jnp.float32) / SMOOTH) ** 2))
     return jnp.where(jnp.abs(offset) <= SMOOTH, values, 0.0)
+
+
+def encode(means):
+    top = functools.reduce(jnp.maximum, [jnp.abs(mean) for mean in means])
+    code = jnp.ceil(jnp.log(jnp.maximum(top, TINY)) * (OCTAVE / math.log(2.0))) + 1.0
+    levels = LEVELS * jnp.exp(code * (-math.log(2.0) / OCTAVE))
+    whole = [jnp.floor(mean * levels + 0.5) for mean in means] + [code]
+    return [value.astype(jnp.int32).astype(jnp.int16) for value in whole]
+
+
+def integer(ref):
+    return ref.astype(jnp.int32).astype(jnp.float32)
+
+
+def scale_of(code):
+    return jnp.exp(integer(code) * (math.log(2.0) / OCTAVE)) * (1.0 / LEVELS)
 
 
 def cycle_kernel(
@@ -87,13 +107,17 @@
     loglik,
     loglik_halo,
     scores,
+    held,
     send,
+    send_log,
     recv,
-    pair,
+    recv_log,
     merged,
     halo_sems,
     send_sems,
     recv_sems,
+    send_log_sems,
+    recv_log_sems,
     back_send,
     back_recv,
     relay_send,
@@ -334,25 +358,33 @@
     partner = me + 1 - 2 * lax.rem(me, 2)
     parity = lax.rem(me, 2)
 
+    half = n // 2
+
+    def copies(t, slot, target):
+        return [
+            pltpu.make_async_remote_copy(
+                src_ref=source.at[t],
+                dst_ref=landing.at[slot],
+                send_sem=sent_sems.at[t],
+                recv_sem=landed_sems.at[slot],
+                device_id={"mem": target},
+                device_id_type=MESH,
+            )
+            for source, landing, sent_sems, landed_sems in (
+                (send_log, recv_log, send_log_sems, recv_log_sems),
+                (send, recv, send_sems, recv_sems),
+            )
+        ]
+
     def outgoing(t):
-        return pltpu.make_async_remote_copy(
-            src_ref=send.at[t],
-            dst_ref=recv.at[me // 2],
-            send_sem=send_sems.at[t],
-            recv_sem=recv_sems.at[me // 2],
-            device_id={"mem": t},
-            device_id_type=MESH,
-        )
+        return copies(t, me // 2, t)
 
     def across_pair(t):
-        return pltpu.make_async_remote_copy(
-            src_ref=send.at[t],
-            dst_ref=pair.at[t // 2],
-            send_sem=send_sems.at[t],
-            recv_sem=recv_sems.at[n // 2 + t // 2],
-            device_id={"mem": partner},
-            device_id_type=MESH,
-        )
+        return copies(t, half + t // 2, partner)
+
+    def start_all(made):
+        for copy in made:
+            copy.start()
 
     def gather(t):
         down, along = tile(t)
@@ -362,43 +394,68 @@
         ]
         peak = functools.reduce(jnp.maximum, live)
         gains = [jnp.exp(score - peak) for score in live]
-        send[t, fields] = functools.reduce(jnp.add, gains)
-        send[t, fields + 1] = peak
-        for kind in range(fields):
-            send[t, kind] = functools.reduce(
+        weighted = [
+            functools.reduce(
                 jnp.add,
                 [
                     gains[slot] * advected[slot, kind, down, along].astype(jnp.float32)
                     for slot in range(slots)
                 ],
             )
+            for kind in range(fields)
+        ]
+        return weighted, functools.reduce(jnp.add, gains), peak
+
+    def put(t, weighted, total, peak):
+        send_log[t] = peak + jnp.log(total)
+        inverse = 1.0 / total
+        for plane, value in enumerate(encode([value * inverse for value in weighted])):
+            send[t, plane] = value
+
+    def hold(t, weighted, total, peak):
+        for plane, value in enumerate(weighted + [total, peak]):
+            held[t // 2, plane] = value
 
     def give_pair(j, carry):
-        t = lax.rem(partner + 4 + 2 * j, owners)
-        gather(t)
-        across_pair(t).start()
-        return carry
+        t = lax.rem(partner + turn(j), owners)
+        put(t, *gather(t))
+        start_all(across_pair(t))
+        return carry
+
+    def turn(j):
+        return lax.rem(owners + 4 - 2 * j, owners)
+
+    def keep_own(j, carry):
+        t = 2 * j + parity
+        hold(t, *gather(t))
+        return carry
+
+    def merge(t, slot):
+        low, high = held[t // 2, fields + 1], recv_log[slot]
+        peak = jnp.maximum(low, high)
+        low, high = jnp.exp(low - peak), jnp.exp(high - peak)
+        scaled = high * scale_of(recv[slot, fields])
+        weighted = [
+            low * held[t // 2, kind] + scaled * integer(recv[slot, kind])
+            for kind in range(fields)
+        ]
+        return weighted, low * held[t // 2, fields] + high, peak
 
     def give_owner(j, carry):
-        t = lax.rem(me + 4 + 2 * j, owners)
-        across_pair(t).wait_recv()
-        low = send[t, fields + 1]
-        high = pair[t // 2, fields + 1]
-        peak = jnp.maximum(low, high)
-        low = jnp.exp(low - peak)
-        high = jnp.exp(high - peak)
-        for kind in range(fields + 1):
-            send[t, kind] = low * send[t, kind] + high * pair[t // 2, kind]
-        send[t, fields + 1] = peak
+        t = lax.rem(me + turn(j), owners)
+        for copy in across_pair(t):
+            copy.wait_recv()
+        sums = merge(t, half + t // 2)
 
         @pl.when(t != me)
         def _():
-            outgoing(t).start()
-
-        return carry
-
-    def keep_own(j, carry):
-        gather(2 * j + parity)
+            put(t, *sums)
+            start_all(outgoing(t))
+
+        @pl.when(t == me)
+        def _():
+            hold(t, *sums)
+
         return carry
 
     lax.fori_loop(0, owners // 2, give_pair, 0)
@@ -429,33 +486,34 @@
     def _():
         def arrive(d, carry):
             source = lax.rem(me + 2 * d, n)
-            pltpu.make_async_remote_copy(
-                src_ref=send.at[0],
-                dst_ref=recv.at[source // 2],
-                send_sem=send_sems.at[0],
-                recv_sem=recv_sems.at[source // 2],
-                device_id={"mem": source},
-                device_id_type=MESH,
-            ).wait_recv()
+            for copy in copies(0, source // 2, source):
+                copy.wait_recv()
             return carry
 
-        lax.fori_loop(1, n // 2, arrive, 0)
-        recv[me // 2] = send[me]
+        lax.fori_loop(1, half, arrive, 0)
+        own = me // 2
         peak = lax.fori_loop(
             1,
-            n // 2,
-            lambda d, top: jnp.maximum(top, recv[d, fields + 1]),
-            recv[0, fields + 1],
+            half,
+            lambda d, top: jnp.maximum(top, recv_log[lax.rem(own + d, half)]),
+            held[own, fields + 1],
         )
 
         def add(d, sums):
-            factor = jnp.exp(recv[d, fields + 1] - peak)
-            return tuple(sums[k] + factor * recv[d, k] for k in range(fields + 1))
-
-        zero = jnp.zeros((TILE_ROWS, TILE_COLS), jnp.float32)
-        sums = lax.fori_loop(0, n // 2, add, (zero,) * (fields + 1))
-        for kind in range(fields):
-            merged[me, kind] = sums[kind] / sums[fields]
+            slot = lax.rem(own + d, half)
+            factor = jnp.exp(recv_log[slot] - peak)
+            scaled = factor * scale_of(recv[slot, fields])
+            return tuple(
+                sums[kind] + scaled * integer(recv[slot, kind]) for kind in range(fields)
+            ) + (sums[fields] + factor,)
+
+        factor = jnp.exp(held[own, fields + 1] - peak)
+        sums = lax.fori_loop(
+            1, half, add, tuple(factor * held[own, plane] for plane in range(fields + 1))
+        )
+        inverse = 1.0 / sums[fields]
+        for plane, value in enumerate(encode([sums[kind] * inverse for kind in range(fields)])):
+            merged[me, plane] = value
 
         def start(d, carry):
             back(d).start()
@@ -483,8 +541,9 @@
 
     def finish(t):
         down, along = tile(t)
+        scale = scale_of(merged[t, fields])
         for kind in range(fields):
-            mean = merged[t, kind]
+            mean = scale * integer(merged[t, kind])
             mean_ref[kind, down, along] = mean.astype(jnp.bfloat16)
             for slot in range(slots):
                 value = advected[slot, kind, down, along].astype(jnp.float32)
@@ -506,11 +565,13 @@
     lax.fori_loop(0, owners, sent, 0)
 
     def passed(j, carry):
-        across_pair(2 * j + 1 - parity).wait_send()
+        for copy in across_pair(2 * j + 1 - parity):
+            copy.wait_send()
 
         @pl.when(2 * j + parity != me)
         def _():
-            outgoing(2 * j + parity).wait_send()
+            for copy in outgoing(2 * j + parity):
+                copy.wait_send()
 
         relay(2 * j + parity).wait_send()
         return carry
@@ -568,13 +629,17 @@
             pltpu.VMEM((slots, rows, width), f32),
             pltpu.VMEM((slots, 16, width), f32),
             pltpu.VMEM((slots, rows, width), f32),
-            pltpu.VMEM((owners, fields + 2, TILE_ROWS, TILE_COLS), f32),
-            pltpu.VMEM((n // 2, fields + 2, TILE_ROWS, TILE_COLS), f32),
-            pltpu.VMEM((owners // 2, fields + 2, TILE_ROWS, TILE_COLS), f32),
-            pltpu.VMEM((owners, fields, TILE_ROWS, TILE_COLS), f32),
+            pltpu.VMEM((owners // 2, fields + 2) + tile, f32),
+            pltpu.VMEM((owners, fields + 1) + tile, jnp.int16),
+            pltpu.VMEM((owners,) + tile, f32),
+            pltpu.VMEM((n // 2 + owners // 2, fields + 1) + tile, jnp.int16),
+            pltpu.VMEM((n // 2 + owners // 2,) + tile, f32),
+            pltpu.VMEM((owners, fields + 1) + tile, jnp.int16),
             pltpu.SemaphoreType.DMA((2, 3)),
             pltpu.SemaphoreType.DMA((owners,)),
-            pltpu.SemaphoreType.DMA((n,)),
+            pltpu.SemaphoreType.DMA((n // 2 + owners // 2,)),
+            pltpu.SemaphoreType.DMA((owners,)),
+            pltpu.SemaphoreType.DMA((n // 2 + owners // 2,)),
             pltpu.SemaphoreType.DMA((n,)),
             pltpu.SemaphoreType.DMA((owners,)),
             pltpu.SemaphoreType.DMA((owners,)),

time: 49.8 us -> 45.1 us (0.906)
  Pallas kernels: 48.3 us -> 43.6 us
    pallas_call x1, Pallas kernels: 47.2 us -> 42.5 us  [cycle(): pl.pallas_call(functools.partial(cycle_kernel, n), out_shape=(pltpu.VMEM(...]
where the time goes in v1:
time: 45.1 us; the launch traced here: 44.8 us
  Pallas kernels  43.6 us (97%)
  between operations  1.29 us (3%)
    pallas_call x1, Pallas kernels, cycle(): pl.pallas_call(functools.partial(cycle_kernel, n), out_shape=(pltpu.VMEM(...  42.5 us
    pallas_call x1, Pallas kernels, write_out(): pl.pallas_call(write_kernel, out_shape=(jax.ShapeDtypeStruct(fresh.shape,...  1.07 us

profile of v1, /device:TPU:0, one launch (start us, length us, event | category | flops | bytes accessed | tf_op | source)
XLA Modules:
  0.0 44.8 jit_solution(9910934470498663386)
XLA Ops:
  1.3 42.5 %shard_map.104 = (bf16[4,8,32,512]{3,2,1,0:T(8,128)(2,1)S(1)}, bf16[8,32,512]{2,1,0:T(8,128)(2,1)S(1)}) custom-call(bf16[4,8,32,512]{3,2,1,0:T(8,128)(2,1)} %state_ref.1, s32[1]{0:T(128)S(6)} %copy.11.counts_ref, f32[32,512]{1,0:T(8,128)} %east_ref.1, f32[32,512]{1,0:T(8,128)} %north_ref.1, s32[1,32768]{1,0:T(1,128)} %cells_ref.1, s32[1,32768]{1,0:T(1,128)} %mask_ref.1, ...), custom_call_target="tpu_custom_call" | custom-call | tf_op jit(solution)/shard_map/pallas_call | solution.py:605
  43.8 1.1 %shard_map.105 = (bf16[4,8,32,512]{3,2,1,0:T(8,128)(2,1)}, bf16[8,32,512]{2,1,0:T(8,128)(2,1)}) custom-call(bf16[4,8,32,512]{3,2,1,0:T(8,128)(2,1)S(1)} %get-tuple-element.4.fresh, bf16[8,32,512]{2,1,0:T(8,128)(2,1)S(1)} %get-tuple-element.5.mean), custom_call_target="tpu_custom_call" | custom-call | tf_op jit(solution)/shard_map/pallas_call | solution.py:671

commit v2 on v1

--- a/solution.py
+++ b/solution.py
@@ -15,6 +15,7 @@
 TILE_ROWS = 16
 TILE_COLS = 128
 OBS_BLOCK = 2048
+TOGETHER = 4
 LEVELS = 32760.0
 OCTAVE = 128.0
 TINY = 1e-33
@@ -55,6 +56,14 @@
     )
 
 
+def one_hot(hit):
+    return jnp.where(hit, 1.0, 0.0).astype(jnp.bfloat16)
+
+
+def permute(values, matrix):
+    return jnp.dot(values, matrix, preferred_element_type=jnp.float32)
+
+
 def kernel_values(offset):
     values = jnp.exp(-((2.0 * offset.astype(jnp.float32) / SMOOTH) ** 2))
     return jnp.where(jnp.abs(offset) <= SMOOTH, values, 0.0)
@@ -94,6 +103,8 @@
     values,
     error,
     state,
+    count,
+    factors,
     counted,
     obs_send,
     obs_recv,
@@ -102,6 +113,10 @@
     wind_in,
     wind_halo,
     winds,
+    spread_columns,
+    gather_columns,
+    lines,
+    moved,
     advected,
     lon_kernel,
     loglik,
@@ -145,6 +160,10 @@
                 (values_ref.at[:, mine], values),
                 (error_ref.at[:, mine], error),
                 (state_ref, state),
+                (east_ref, wind_in.at[0]),
+                (north_ref, wind_in.at[1]),
+                (counts_ref, count),
+                (relax_ref, factors),
             )
         )
     ]
@@ -162,13 +181,15 @@
     pl.semaphore_signal(barrier, inc=1, device_id={"lat": other}, device_id_type=MESH)
     lax.fori_loop(1, n, greet, 0)
 
-    wind_in[0] = east_ref[...]
-    wind_in[1] = north_ref[...]
     i0 = lax.broadcasted_iota(jnp.int32, (width, width), 0)
     i1 = lax.broadcasted_iota(jnp.int32, (width, width), 1)
+    spread_columns[...] = one_hot(i0 == across * lax.rem(i1, TILE_COLS) + i1 // TILE_COLS)
+    gather_columns[...] = one_hot(i1 == across * lax.rem(i0, TILE_COLS) + i0 // TILE_COLS)
     apart = jnp.abs(i0 - i1)
     lon_kernel[...] = kernel_values(jnp.minimum(apart, width - apart))
 
+    for load in loads[5:]:
+        load.wait()
     pl.semaphore_wait(barrier, n)
 
     def to_other(source, target, slot):
@@ -251,40 +272,89 @@
     near = lax.broadcasted_iota(jnp.int32, (8, width), 0)
     keep = jnp.where(band == 0, near, 7 - near) < STEPS
 
+    layers = (rows + 8) // 8
+
+    def columns(c):
+        return slice(c * TILE_COLS, (c + 1) * TILE_COLS)
+
+    def spread(ref, c):
+        return jnp.stack([ref[c, pl.ds(k, 8, stride=layers), :] for k in range(layers)])
+
     copy_winds.wait()
+    split = []
     for kind in range(2):
-        own = wind_in[kind]
         far = jnp.where(keep, wind_halo[kind], 0.0)
-        whole = jnp.concatenate([own, far], axis=0)
-        winds[2 * kind] = jnp.abs(whole)
-        winds[2 * kind + 1] = whole
+        split += pieces(jnp.concatenate([wind_in[kind], far], axis=0))
+    split = permute(
+        jnp.concatenate([piece.astype(jnp.bfloat16) for piece in split], axis=0),
+        spread_columns[...],
+    ).reshape(2, 3, rows + 8, width)
+    for kind in range(2):
+        whole = (split[kind, 0] + split[kind, 1]) + split[kind, 2]
+        for c in range(across):
+            lines[0, kind, c] = whole[:, columns(c)]
+            wind = spread(lines.at[0, kind], c)
+            winds[2 * kind, c] = jnp.abs(wind)
+            winds[2 * kind + 1, c] = wind
     loads[4].wait()
     copy_state.wait()
 
+    def lay_out(slot, carry):
+        whole = permute(
+            jnp.concatenate(
+                [state[slot].reshape(fields * rows, width), halo[slot].reshape(fields * 16, width)],
+                axis=0,
+            ),
+            spread_columns[...],
+        )
+        own = whole[: fields * rows].reshape(fields, rows, width)
+        far = whole[fields * rows :].reshape(fields, 16, width)
+        far = jnp.where(band == 0, far[:, :8], far[:, 8:])
+        for c in range(across):
+            lines[slot, :, c, :rows] = own[:, :, columns(c)]
+            lines[slot, :, c, rows:] = jnp.where(keep[:, columns(c)], far[:, :, columns(c)], 0.0)
+        return carry
+
+    lax.fori_loop(0, slots, lay_out, 0)
+
+    def step(x):
+        west = [pltpu.roll(x[across - 1], 1, 2)] + x[:-1]
+        east = x[1:] + [pltpu.roll(x[0], TILE_COLS - 1, 2)]
+        south = [
+            jnp.concatenate([pltpu.roll(v[layers - 1 :], 1, 1), v[: layers - 1]], axis=0) for v in x
+        ]
+        north = [jnp.concatenate([v[1:], pltpu.roll(v[:1], 7, 1)], axis=0) for v in x]
+        return [
+            x[c]
+            - winds[0, c] * (x[c] - jnp.where(winds[1, c] > 0.0, west[c], east[c]))
+            - winds[2, c] * (x[c] - jnp.where(winds[3, c] > 0.0, south[c], north[c]))
+            for c in range(across)
+        ]
+
     def move(index, carry):
-        kind = index // slots
-        slot = lax.rem(index, slots)
-        own = state[slot, kind].astype(jnp.float32)
-        far = halo[slot, kind].astype(jnp.float32)
-        far = jnp.where(band == 0, far[:8], far[8:])
-        far = jnp.where(keep, far, 0.0)
-        x = jnp.concatenate([own, far], axis=0)
+        kind = index // (slots // TOGETHER)
+        first = TOGETHER * lax.rem(index, slots // TOGETHER)
+        fields_of = [lines.at[first + k, kind] for k in range(TOGETHER)]
+        xs = [[spread(field, c) for c in range(across)] for field in fields_of]
         for _ in range(STEPS):
-            west = pltpu.roll(x, 1, 1)
-            east = pltpu.roll(x, width - 1, 1)
-            south = pltpu.roll(x, 1, 0)
-            north = pltpu.roll(x, rows + 7, 0)
-            x = (
-                x
-                - winds[0] * (x - jnp.where(winds[1] > 0.0, west, east))
-                - winds[2] * (x - jnp.where(winds[3] > 0.0, south, north))
-            )
-        advected[slot, kind] = x[:rows].astype(jnp.bfloat16)
-        return carry
-
-    total = slots * fields
+            xs = [step(x) for x in xs]
+        for k, (field, x) in enumerate(zip(fields_of, xs)):
+            for c in range(across):
+                for layer in range(layers):
+                    field[c, pl.ds(layer, 8, stride=layers), :] = x[c][layer]
+                moved[kind, first + k, :, columns(c)] = field[c, :rows].astype(jnp.bfloat16)
+        return carry
+
+    def collect(first, last):
+        whole = moved[first:last].reshape((last - first) * slots * rows, width)
+        whole = permute(whole, gather_columns[...]).astype(jnp.bfloat16)
+        advected[first:last] = whole.reshape(last - first, slots, rows, width)
+
+    total = fields * (slots // TOGETHER)
     early, late = 3 * total // 8, 6 * total // 8
-    lax.fori_loop(0, early, move, 0)
+    lax.fori_loop(0, slots // TOGETHER, move, 0)
+    collect(0, 1)
+    lax.fori_loop(slots // TOGETHER, early, move, 0)
 
     @pl.when(me < owners)
     def _():
@@ -326,7 +396,7 @@
 
         down, along = tile(t)
         for slot in range(slots):
-            value = advected[slot, 0, down, along].astype(jnp.float32)
+            value = advected[0, slot, down, along].astype(jnp.float32)
             loglik[slot, down, along] = -0.5 * (
                 grids[t, 0] * value * value - 2.0 * grids[t, 1] * value + grids[t, 2]
             )
@@ -335,6 +405,7 @@
     lax.fori_loop(0, owners, likely, 0)
     copy_loglik = to_other(loglik.at[:, edge16, :], loglik_halo, 2)
     lax.fori_loop(late, total, move, 0)
+    collect(1, fields)
 
     r0 = lax.broadcasted_iota(jnp.int32, (rows, rows), 0)
     r1 = lax.broadcasted_iota(jnp.int32, (rows, rows), 1)
@@ -389,7 +460,7 @@
     def gather(t):
         down, along = tile(t)
         live = [
-            jnp.where(slot < counts_ref[0], scores[slot, down, along], -jnp.inf)
+            jnp.where(slot < count[0], scores[slot, down, along], -jnp.inf)
             for slot in range(slots)
         ]
         peak = functools.reduce(jnp.maximum, live)
@@ -398,7 +469,7 @@
             functools.reduce(
                 jnp.add,
                 [
-                    gains[slot] * advected[slot, kind, down, along].astype(jnp.float32)
+                    gains[slot] * advected[kind, slot, down, along].astype(jnp.float32)
                     for slot in range(slots)
                 ],
             )
@@ -416,14 +487,16 @@
         for plane, value in enumerate(weighted + [total, peak]):
             held[t // 2, plane] = value
 
+    def turn(j):
+        middle = owners // 2
+        other_ones = 2 * j + 2 * jnp.where(2 * j >= middle, 1, 0)
+        return jnp.where(j == 0, middle, jnp.where(j == middle - 1, 0, other_ones))
+
     def give_pair(j, carry):
         t = lax.rem(partner + turn(j), owners)
         put(t, *gather(t))
         start_all(across_pair(t))
         return carry
-
-    def turn(j):
-        return lax.rem(owners + 4 - 2 * j, owners)
 
     def keep_own(j, carry):
         t = 2 * j + parity
@@ -546,10 +619,10 @@
             mean = scale * integer(merged[t, kind])
             mean_ref[kind, down, along] = mean.astype(jnp.bfloat16)
             for slot in range(slots):
-                value = advected[slot, kind, down, along].astype(jnp.float32)
-                fresh = value + relax_ref[kind] * (mean - value)
+                value = advected[kind, slot, down, along].astype(jnp.float32)
+                fresh = value + factors[kind] * (mean - value)
                 out_ref[slot, kind, down, along] = jnp.where(
-                    slot < counts_ref[0], fresh, 0.0
+                    slot < count[0], fresh, 0.0
                 ).astype(jnp.bfloat16)
 
     lax.fori_loop(0, owners // 2, pass_on, 0)
@@ -595,12 +668,12 @@
 
 def cycle(n, state, counts, east_wind, north_wind, obs, relax):
     slots, fields, rows, width = state.shape
-    owners = (rows // TILE_ROWS) * (width // TILE_COLS)
+    across = width // TILE_COLS
+    owners = (rows // TILE_ROWS) * across
     share = obs[0].shape[1] // n
     tile = (TILE_ROWS, TILE_COLS)
     hbm = pl.BlockSpec(memory_space=pl.ANY)
     vmem = pl.BlockSpec(memory_space=pltpu.VMEM)
-    smem = pl.BlockSpec(memory_space=pltpu.SMEM)
     f32, bf16 = jnp.float32, jnp.bfloat16
     return pl.pallas_call(
         functools.partial(cycle_kernel, n),
@@ -608,7 +681,7 @@
             pltpu.VMEM(state.shape, bf16),
             pltpu.VMEM((fields, rows, width), bf16),
         ),
-        in_specs=[hbm, smem, vmem, vmem, hbm, hbm, hbm, hbm, smem],
+        in_specs=[hbm] * 9,
         out_specs=(vmem, vmem),
         scratch_shapes=[
             pltpu.VMEM((1, share), jnp.int32),
@@ -616,6 +689,8 @@
             pltpu.VMEM((1, share), f32),
             pltpu.VMEM((1, share), f32),
             pltpu.VMEM(state.shape, bf16),
+            pltpu.SMEM(counts.shape, counts.dtype),
+            pltpu.SMEM(relax.shape, relax.dtype),
             pltpu.VMEM((3, rows, width), f32),
             pltpu.VMEM((owners, 3) + tile, f32),
             pltpu.VMEM((n, 3) + tile, f32),
@@ -623,8 +698,12 @@
             pltpu.VMEM((slots, fields, 16, width), bf16),
             pltpu.VMEM((2, rows, width), f32),
             pltpu.VMEM((2, 8, width), f32),
-            pltpu.VMEM((4, rows + 8, width), f32),
-            pltpu.VMEM((slots, fields, rows, width), bf16),
+            pltpu.VMEM((4, across, (rows + 8) // 8, 8, TILE_COLS), f32),
+            pltpu.VMEM((width, width), bf16),
+            pltpu.VMEM((width, width), bf16),
+            pltpu.VMEM((slots, fields, across, rows + 8, TILE_COLS), f32),
+            pltpu.VMEM((fields, slots, rows, width), bf16),
+            pltpu.VMEM((fields, slots, rows, width), bf16),
             pltpu.VMEM((width, width), f32),
             pltpu.VMEM((slots, rows, width), f32),
             pltpu.VMEM((slots, 16, width), f32),
@@ -643,7 +722,7 @@
             pltpu.SemaphoreType.DMA((n,)),
             pltpu.SemaphoreType.DMA((owners,)),
             pltpu.SemaphoreType.DMA((owners,)),
-            pltpu.SemaphoreType.DMA((5,)),
+            pltpu.SemaphoreType.DMA((9,)),
             pltpu.SemaphoreType.DMA((owners,)),
             pltpu.SemaphoreType.DMA((n,)),
             pltpu.SemaphoreType.DMA((n,)),

time: 45.1 us -> 41.7 us (0.925)
  Pallas kernels: 43.6 us -> 40.2 us
    pallas_call x1, Pallas kernels: 42.5 us -> 39.2 us  [cycle(): pl.pallas_call(functools.partial(cycle_kernel, n), out_shape=(pltpu.VMEM(...]
where the time goes in v2:
time: 41.7 us; the launch traced here: 41.5 us
  Pallas kernels  40.2 us (96%)
  between operations  1.29 us (3%)
    pallas_call x1, Pallas kernels, cycle(): pl.pallas_call(functools.partial(cycle_kernel, n), out_shape=(pltpu.VMEM(...  39.2 us
    pallas_call x1, Pallas kernels, write_out(): pl.pallas_call(write_kernel, out_shape=(jax.ShapeDtypeStruct(fresh.shape,...  1.07 us

profile of v2, /device:TPU:0, one launch (start us, length us, event | category | flops | bytes accessed | tf_op | source)
XLA Modules:
  0.0 41.5 jit_solution(12298978101501867370)
XLA Ops:
  1.3 39.2 %shard_map.104 = (bf16[4,8,32,512]{3,2,1,0:T(8,128)(2,1)S(1)}, bf16[8,32,512]{2,1,0:T(8,128)(2,1)S(1)}) custom-call(bf16[4,8,32,512]{3,2,1,0:T(8,128)(2,1)} %state_ref.1, s32[1]{0:T(128)S(6)} %copy.11.counts_ref, f32[32,512]{1,0:T(8,128)} %east_ref.1, f32[32,512]{1,0:T(8,128)} %north_ref.1, s32[1,32768]{1,0:T(1,128)} %cells_ref.1, s32[1,32768]{1,0:T(1,128)} %mask_ref.1, ...), custom_call_target="tpu_custom_call" | custom-call | tf_op jit(solution)/shard_map/pallas_call | solution.py:678
  40.4 1.1 %shard_map.105 = (bf16[4,8,32,512]{3,2,1,0:T(8,128)(2,1)}, bf16[8,32,512]{2,1,0:T(8,128)(2,1)}) custom-call(bf16[4,8,32,512]{3,2,1,0:T(8,128)(2,1)S(1)} %get-tuple-element.4.fresh, bf16[8,32,512]{2,1,0:T(8,128)(2,1)S(1)} %get-tuple-element.5.mean), custom_call_target="tpu_custom_call" | custom-call | tf_op jit(solution)/shard_map/pallas_call | solution.py:750

commit v3 on v2

--- a/solution.py
+++ b/solution.py
@@ -16,6 +16,7 @@
 TILE_COLS = 128
 OBS_BLOCK = 2048
 TOGETHER = 4
+SHARERS = 4
 LEVELS = 32760.0
 OCTAVE = 128.0
 TINY = 1e-33
@@ -46,8 +47,7 @@
     left = jnp.concatenate(
         [
             jnp.where(row_hit, piece, 0.0).astype(jnp.bfloat16)
-            for term in terms
-            for piece in pieces(term)
+            for piece in pieces(terms[0]) + pieces(terms[1]) + pieces(terms[2])[:2]
         ],
         axis=0,
     )
@@ -150,7 +150,9 @@
     other = 1 - band
 
     share = cells.shape[1]
-    mine = pl.ds(pl.multiple_of(me * share, 128), share)
+    rank = lax.rem(me, SHARERS)
+    first_rank = me - rank
+    mine = pl.ds(pl.multiple_of(rank * share, 128), share)
     loads = [
         pltpu.make_async_copy(source, target, local_sems.at[k])
         for k, (source, target) in enumerate(
@@ -181,13 +183,6 @@
     pl.semaphore_signal(barrier, inc=1, device_id={"lat": other}, device_id_type=MESH)
     lax.fori_loop(1, n, greet, 0)
 
-    i0 = lax.broadcasted_iota(jnp.int32, (width, width), 0)
-    i1 = lax.broadcasted_iota(jnp.int32, (width, width), 1)
-    spread_columns[...] = one_hot(i0 == across * lax.rem(i1, TILE_COLS) + i1 // TILE_COLS)
-    gather_columns[...] = one_hot(i1 == across * lax.rem(i0, TILE_COLS) + i0 // TILE_COLS)
-    apart = jnp.abs(i0 - i1)
-    lon_kernel[...] = kernel_values(jnp.minimum(apart, width - apart))
-
     for load in loads[5:]:
         load.wait()
     pl.semaphore_wait(barrier, n)
@@ -219,55 +214,63 @@
     for load in loads[:4]:
         load.wait()
     block = min(share, OBS_BLOCK)
-    for start in range(0, share, block):
-        part = partial_grids(
-            rows, width, *(ref[:, start : start + block] for ref in (cells, mask, values, error))
-        )
-        for term in range(3):
-            base = 3 * term * rows
-            terms = (
-                part[base : base + rows]
-                + part[base + rows : base + 2 * rows]
-                + part[base + 2 * rows : base + 3 * rows]
+
+    def count_block(index, carry):
+        at = pl.ds(pl.multiple_of(index * block, 128), block)
+        part = partial_grids(rows, width, *(ref[:, at] for ref in (cells, mask, values, error)))
+        for term, (base, number) in enumerate(((0, 3), (3, 3), (6, 2))):
+            counted[term] += functools.reduce(
+                jnp.add, [part[(base + k) * rows : (base + k + 1) * rows] for k in range(number)]
             )
-            if start == 0:
-                counted[term] = terms
-            else:
-                counted[term] += terms
-
-    def obs_out(t):
+        return carry
+
+    counted[...] = jnp.zeros_like(counted)
+    lax.fori_loop(0, share // block, count_block, 0)
+    held_tiles = owners // SHARERS
+
+    def near_by(d):
+        return lax.rem(rank + d, SHARERS)
+
+    def obs_out(d):
         return pltpu.make_async_remote_copy(
-            src_ref=obs_send.at[t],
-            dst_ref=obs_recv.at[me],
-            send_sem=obs_sems.at[t],
-            recv_sem=obs_arrived.at[me],
-            device_id={"mem": t},
+            src_ref=obs_send.at[near_by(d)],
+            dst_ref=obs_recv.at[rank],
+            send_sem=obs_sems.at[near_by(d)],
+            recv_sem=obs_arrived.at[rank],
+            device_id={"mem": first_rank + near_by(d)},
             device_id_type=MESH,
         )
 
-    def give(j, carry):
-        t = lax.rem(me + 1 + j, owners)
-        down, along = tile(t)
-        for term in range(3):
-            obs_send[t, term] = counted[term, down, along]
-
-        @pl.when(t != me)
+    def give(d, carry):
+        for k in range(held_tiles):
+            down, along = tile(held_tiles * near_by(d) + k)
+            for term in range(3):
+                obs_send[near_by(d), k, term] = counted[term, down, along]
+
+        @pl.when(d < SHARERS)
         def _():
-            obs_out(t).start()
-
-        return carry
-
-    lax.fori_loop(0, owners, give, 0)
+            obs_out(d).start()
+
+        return carry
+
+    lax.fori_loop(1, SHARERS + 1, give, 0)
 
     def grid_out(d):
         return pltpu.make_async_remote_copy(
-            src_ref=grids.at[me],
-            dst_ref=grids.at[me],
+            src_ref=grids.at[rank],
+            dst_ref=grids.at[rank],
             send_sem=grid_sems.at[d],
-            recv_sem=grid_arrived.at[me],
-            device_id={"mem": lax.rem(me + d, n)},
+            recv_sem=grid_arrived.at[rank],
+            device_id={"mem": first_rank + near_by(d)},
             device_id_type=MESH,
         )
+
+    i0 = lax.broadcasted_iota(jnp.int32, (width, width), 0)
+    i1 = lax.broadcasted_iota(jnp.int32, (width, width), 1)
+    spread_columns[...] = one_hot(i0 == across * lax.rem(i1, TILE_COLS) + i1 // TILE_COLS)
+    gather_columns[...] = one_hot(i1 == across * lax.rem(i0, TILE_COLS) + i0 // TILE_COLS)
+    apart = jnp.abs(i0 - i1)
+    lon_kernel[...] = kernel_values(jnp.minimum(apart, width - apart))
 
     near = lax.broadcasted_iota(jnp.int32, (8, width), 0)
     keep = jnp.where(band == 0, near, 7 - near) < STEPS
@@ -356,53 +359,51 @@
     collect(0, 1)
     lax.fori_loop(slots // TOGETHER, early, move, 0)
 
-    @pl.when(me < owners)
-    def _():
-        def arrive(d, carry):
-            source = lax.rem(me + n - d, n)
+    def arrive(d, carry):
+        source = near_by(SHARERS - d)
+        pltpu.make_async_remote_copy(
+            src_ref=obs_send.at[0],
+            dst_ref=obs_recv.at[source],
+            send_sem=obs_sems.at[0],
+            recv_sem=obs_arrived.at[source],
+            device_id={"mem": first_rank + source},
+            device_id_type=MESH,
+        ).wait_recv()
+        return carry
+
+    lax.fori_loop(1, SHARERS, arrive, 0)
+    obs_recv[rank] = obs_send[rank]
+    grids[rank] = functools.reduce(jnp.add, [obs_recv[k] for k in range(SHARERS)])
+    for d in range(1, SHARERS):
+        grid_out(d).start()
+
+    lax.fori_loop(early, late, move, 0)
+
+    def likely(d, carry):
+        source = near_by(d)
+
+        @pl.when(d > 0)
+        def _():
             pltpu.make_async_remote_copy(
-                src_ref=obs_send.at[0],
-                dst_ref=obs_recv.at[source],
-                send_sem=obs_sems.at[0],
-                recv_sem=obs_arrived.at[source],
-                device_id={"mem": source},
+                src_ref=grids.at[source],
+                dst_ref=grids.at[source],
+                send_sem=grid_sems.at[0],
+                recv_sem=grid_arrived.at[source],
+                device_id={"mem": first_rank + source},
                 device_id_type=MESH,
             ).wait_recv()
-            return carry
-
-        lax.fori_loop(1, n, arrive, 0)
-        obs_recv[me] = obs_send[me]
-        grids[me] = lax.fori_loop(1, n, lambda d, sums: sums + obs_recv[d], obs_recv[0])
-
-        def start(d, carry):
-            grid_out(d).start()
-            return carry
-
-        lax.fori_loop(1, n, start, 0)
-
-    lax.fori_loop(early, late, move, 0)
-
-    def likely(t, carry):
-        @pl.when(t != me)
-        def _():
-            pltpu.make_async_remote_copy(
-                src_ref=grids.at[t],
-                dst_ref=grids.at[t],
-                send_sem=grid_sems.at[0],
-                recv_sem=grid_arrived.at[t],
-                device_id={"mem": t},
-                device_id_type=MESH,
-            ).wait_recv()
-
-        down, along = tile(t)
-        for slot in range(slots):
-            value = advected[0, slot, down, along].astype(jnp.float32)
-            loglik[slot, down, along] = -0.5 * (
-                grids[t, 0] * value * value - 2.0 * grids[t, 1] * value + grids[t, 2]
-            )
-        return carry
-
-    lax.fori_loop(0, owners, likely, 0)
+
+        for k in range(held_tiles):
+            down, along = tile(held_tiles * source + k)
+            inverse, linear, constant = (grids[source, k, term] for term in range(3))
+            for slot in range(slots):
+                value = advected[0, slot, down, along].astype(jnp.float32)
+                loglik[slot, down, along] = -0.5 * (
+                    inverse * value * value - 2.0 * linear * value + constant
+                )
+        return carry
+
+    lax.fori_loop(0, SHARERS, likely, 0)
     copy_loglik = to_other(loglik.at[:, edge16, :], loglik_halo, 2)
     lax.fori_loop(late, total, move, 0)
     collect(1, fields)
@@ -628,14 +629,9 @@
     lax.fori_loop(0, owners // 2, pass_on, 0)
     lax.fori_loop(0, owners // 2, accept, 0)
 
-    def sent(t, carry):
-        @pl.when(t != me)
-        def _():
-            obs_out(t).wait_send()
-
-        return carry
-
-    lax.fori_loop(0, owners, sent, 0)
+    for d in range(1, SHARERS):
+        obs_out(d).wait_send()
+        grid_out(d).wait_send()
 
     def passed(j, carry):
         for copy in across_pair(2 * j + 1 - parity):
@@ -659,18 +655,13 @@
 
         lax.fori_loop(1, n // 2, sent_back, 0)
 
-        def sent_grids(d, carry):
-            grid_out(d).wait_send()
-            return carry
-
-        lax.fori_loop(1, n, sent_grids, 0)
-
 
 def cycle(n, state, counts, east_wind, north_wind, obs, relax):
     slots, fields, rows, width = state.shape
     across = width // TILE_COLS
     owners = (rows // TILE_ROWS) * across
-    share = obs[0].shape[1] // n
+    share = obs[0].shape[1] // SHARERS
+    held_tiles = owners // SHARERS
     tile = (TILE_ROWS, TILE_COLS)
     hbm = pl.BlockSpec(memory_space=pl.ANY)
     vmem = pl.BlockSpec(memory_space=pltpu.VMEM)
@@ -692,9 +683,9 @@
             pltpu.SMEM(counts.shape, counts.dtype),
             pltpu.SMEM(relax.shape, relax.dtype),
             pltpu.VMEM((3, rows, width), f32),
-            pltpu.VMEM((owners, 3) + tile, f32),
-            pltpu.VMEM((n, 3) + tile, f32),
-            pltpu.VMEM((owners, 3) + tile, f32),
+            pltpu.VMEM((SHARERS, held_tiles, 3) + tile, f32),
+            pltpu.VMEM((SHARERS, held_tiles, 3) + tile, f32),
+            pltpu.VMEM((SHARERS, held_tiles, 3) + tile, f32),
             pltpu.VMEM((slots, fields, 16, width), bf16),
             pltpu.VMEM((2, rows, width), f32),
             pltpu.VMEM((2, 8, width), f32),
@@ -723,10 +714,10 @@
             pltpu.SemaphoreType.DMA((owners,)),
             pltpu.SemaphoreType.DMA((owners,)),
             pltpu.SemaphoreType.DMA((9,)),
-            pltpu.SemaphoreType.DMA((owners,)),
-            pltpu.SemaphoreType.DMA((n,)),
-            pltpu.SemaphoreType.DMA((n,)),
-            pltpu.SemaphoreType.DMA((owners,)),
+            pltpu.SemaphoreType.DMA((SHARERS,)),
+            pltpu.SemaphoreType.DMA((SHARERS,)),
+            pltpu.SemaphoreType.DMA((SHARERS,)),
+            pltpu.SemaphoreType.DMA((SHARERS,)),
         ],
         compiler_params=pltpu.CompilerParams(
             collective_id=0, has_side_effects=True, vmem_limit_bytes=56 * 1024 * 1024

time: 41.7 us -> 39.8 us (0.954)
  Pallas kernels: 40.2 us -> 38.4 us
    pallas_call x1, Pallas kernels: 39.2 us -> 37.3 us  [cycle(): pl.pallas_call(functools.partial(cycle_kernel, n), out_shape=(pltpu.VMEM(...]
where the time goes in v3:
time: 39.8 us; the launch traced here: 39.7 us
  Pallas kernels  38.4 us (96%)
  between operations  1.29 us (3%)
    pallas_call x1, Pallas kernels, cycle(): pl.pallas_call(functools.partial(cycle_kernel, n), out_shape=(pltpu.VMEM(...  37.3 us
    pallas_call x1, Pallas kernels, write_out(): pl.pallas_call(write_kernel, out_shape=(jax.ShapeDtypeStruct(fresh.shape,...  1.07 us

profile of v3, /device:TPU:0, one launch (start us, length us, event | category | flops | bytes accessed | tf_op | source)
XLA Modules:
  0.0 39.7 jit_solution(3248425939118468339)
XLA Ops:
  1.3 37.3 %shard_map.104 = (bf16[4,8,32,512]{3,2,1,0:T(8,128)(2,1)S(1)}, bf16[8,32,512]{2,1,0:T(8,128)(2,1)S(1)}) custom-call(bf16[4,8,32,512]{3,2,1,0:T(8,128)(2,1)} %state_ref.1, s32[1]{0:T(128)S(6)} %copy.11.counts_ref, f32[32,512]{1,0:T(8,128)} %east_ref.1, f32[32,512]{1,0:T(8,128)} %north_ref.1, s32[1,32768]{1,0:T(1,128)} %cells_ref.1, s32[1,32768]{1,0:T(1,128)} %mask_ref.1, ...), custom_call_target="tpu_custom_call" | custom-call | tf_op jit(solution)/shard_map/pallas_call | solution.py:669
  38.6 1.1 %shard_map.105 = (bf16[4,8,32,512]{3,2,1,0:T(8,128)(2,1)}, bf16[8,32,512]{2,1,0:T(8,128)(2,1)}) custom-call(bf16[4,8,32,512]{3,2,1,0:T(8,128)(2,1)S(1)} %get-tuple-element.4.fresh, bf16[8,32,512]{2,1,0:T(8,128)(2,1)S(1)} %get-tuple-element.5.mean), custom_call_target="tpu_custom_call" | custom-call | tf_op jit(solution)/shard_map/pallas_call | solution.py:741

commit v4 on v3

--- a/solution.py
+++ b/solution.py
@@ -354,7 +354,7 @@
         advected[first:last] = whole.reshape(last - first, slots, rows, width)
 
     total = fields * (slots // TOGETHER)
-    early, late = 3 * total // 8, 6 * total // 8
+    early, late = total // 8, 7 * total // 8
     lax.fori_loop(0, slots // TOGETHER, move, 0)
     collect(0, 1)
     lax.fori_loop(slots // TOGETHER, early, move, 0)
@@ -488,10 +488,18 @@
         for plane, value in enumerate(weighted + [total, peak]):
             held[t // 2, plane] = value
 
+    middle = owners // 2
+    place = lax.rem(me // 2, middle)
+
+    def near_to_far(k):
+        ups, downs = middle - 1 - place, place
+        both = jnp.minimum(ups, downs)
+        upward = jnp.where(ups > downs, k - both, 0 - (k - both))
+        paired = jnp.where(lax.rem(k, 2) == 1, (k + 1) // 2, 0 - (k // 2))
+        return lax.rem(jnp.where(k <= 2 * both, paired, upward) + middle, middle)
+
     def turn(j):
-        middle = owners // 2
-        other_ones = 2 * j + 2 * jnp.where(2 * j >= middle, 1, 0)
-        return jnp.where(j == 0, middle, jnp.where(j == middle - 1, 0, other_ones))
+        return 2 * near_to_far(middle - 1 - j)
 
     def give_pair(j, carry):
         t = lax.rem(partner + turn(j), owners)
@@ -593,22 +601,28 @@
             back(d).start()
             return carry
 
-        lax.fori_loop(1, n // 2, start, 0)
+        lax.fori_loop(1, half, start, 0)
 
     def landed(t):
         @pl.when(t != me)
         def _():
             relay(t).wait_recv()
 
-    def pass_on(j, carry):
-        t = lax.rem(me + owners - 2 * j, owners)
+    def place_of(start, k):
+        return lax.rem(start + 2 * near_to_far(k), owners)
+
+    def pass_on(k, carry):
+        t = place_of(me, k)
         landed(t)
         relay(t).start()
-        finish(t)
-        return carry
-
-    def accept(j, carry):
-        t = lax.rem(partner + owners - 2 * j, owners)
+        return carry
+
+    def finish_passed(k, carry):
+        finish(place_of(me, k))
+        return carry
+
+    def accept(k, carry):
+        t = place_of(partner, k)
         landed(t)
         finish(t)
         return carry
@@ -626,9 +640,6 @@
                     slot < count[0], fresh, 0.0
                 ).astype(jnp.bfloat16)
 
-    lax.fori_loop(0, owners // 2, pass_on, 0)
-    lax.fori_loop(0, owners // 2, accept, 0)
-
     for d in range(1, SHARERS):
         obs_out(d).wait_send()
         grid_out(d).wait_send()
@@ -642,10 +653,20 @@
             for copy in outgoing(2 * j + parity):
                 copy.wait_send()
 
+        return carry
+
+    lax.fori_loop(0, owners // 2, passed, 0)
+    pass_on(0, 0)
+    finish(place_of(me, 0))
+    lax.fori_loop(1, middle, pass_on, 0)
+    lax.fori_loop(1, middle, finish_passed, 0)
+    lax.fori_loop(0, middle, accept, 0)
+
+    def relayed(j, carry):
         relay(2 * j + parity).wait_send()
         return carry
 
-    lax.fori_loop(0, owners // 2, passed, 0)
+    lax.fori_loop(0, middle, relayed, 0)
 
     @pl.when(me < owners)
     def _():

time: 39.8 us -> 38.6 us (0.970)
  Pallas kernels: 38.4 us -> 37.1 us
    pallas_call x1, Pallas kernels: 37.3 us -> 36.1 us  [cycle(): pl.pallas_call(functools.partial(cycle_kernel, n), out_shape=(pltpu.VMEM(...]
where the time goes in v4:
time: 38.6 us; the launch traced here: 38.4 us
  Pallas kernels  37.1 us (96%)
  between operations  1.29 us (3%)
    pallas_call x1, Pallas kernels, cycle(): pl.pallas_call(functools.partial(cycle_kernel, n), out_shape=(pltpu.VMEM(...  36.1 us
    pallas_call x1, Pallas kernels, write_out(): pl.pallas_call(write_kernel, out_shape=(jax.ShapeDtypeStruct(fresh.shape,...  1.07 us

profile of v4, /device:TPU:0, one launch (start us, length us, event | category | flops | bytes accessed | tf_op | source)
XLA Modules:
  0.0 38.4 jit_solution(8617615552648673844)
XLA Ops:
  1.3 36.1 %shard_map.104 = (bf16[4,8,32,512]{3,2,1,0:T(8,128)(2,1)S(1)}, bf16[8,32,512]{2,1,0:T(8,128)(2,1)S(1)}) custom-call(bf16[4,8,32,512]{3,2,1,0:T(8,128)(2,1)} %state_ref.1, s32[1]{0:T(128)S(6)} %copy.11.counts_ref, f32[32,512]{1,0:T(8,128)} %east_ref.1, f32[32,512]{1,0:T(8,128)} %north_ref.1, s32[1,32768]{1,0:T(1,128)} %cells_ref.1, s32[1,32768]{1,0:T(1,128)} %mask_ref.1, ...), custom_call_target="tpu_custom_call" | custom-call | tf_op jit(solution)/shard_map/pallas_call | solution.py:690
  37.3 1.1 %shard_map.105 = (bf16[4,8,32,512]{3,2,1,0:T(8,128)(2,1)}, bf16[8,32,512]{2,1,0:T(8,128)(2,1)}) custom-call(bf16[4,8,32,512]{3,2,1,0:T(8,128)(2,1)S(1)} %get-tuple-element.4.fresh, bf16[8,32,512]{2,1,0:T(8,128)(2,1)S(1)} %get-tuple-element.5.mean), custom_call_target="tpu_custom_call" | custom-call | tf_op jit(solution)/shard_map/pallas_call | solution.py:762

commit v5 on v4

--- a/solution.py
+++ b/solution.py
@@ -14,7 +14,7 @@
 MESH = pl.DeviceIdType.MESH
 TILE_ROWS = 16
 TILE_COLS = 128
-OBS_BLOCK = 2048
+OBS_BLOCK = 4096
 TOGETHER = 4
 SHARERS = 4
 LEVELS = 32760.0
@@ -229,7 +229,12 @@
     held_tiles = owners // SHARERS
 
     def near_by(d):
-        return lax.rem(rank + d, SHARERS)
+        one_on = rank + 1 - 2 * lax.rem(rank, 2)
+        across_block = lax.rem(rank + SHARERS // 2, SHARERS)
+        opposite = SHARERS - 1 - rank
+        return jnp.where(
+            d == 1, opposite, jnp.where(d == 2, across_block, jnp.where(d == 3, one_on, rank))
+        )
 
     def obs_out(d):
         return pltpu.make_async_remote_copy(
@@ -360,7 +365,7 @@
     lax.fori_loop(slots // TOGETHER, early, move, 0)
 
     def arrive(d, carry):
-        source = near_by(SHARERS - d)
+        source = near_by(d)
         pltpu.make_async_remote_copy(
             src_ref=obs_send.at[0],
             dst_ref=obs_recv.at[source],
@@ -380,7 +385,7 @@
     lax.fori_loop(early, late, move, 0)
 
     def likely(d, carry):
-        source = near_by(d)
+        source = near_by(SHARERS - d)
 
         @pl.when(d > 0)
         def _():

time: 38.6 us -> 38.1 us (0.987)
  Pallas kernels: 37.1 us -> 36.7 us
    pallas_call x1, Pallas kernels: 36.1 us -> 35.6 us  [cycle(): pl.pallas_call(functools.partial(cycle_kernel, n), out_shape=(pltpu.VMEM(...]
where the time goes in v5:
time: 38.1 us; the launch traced here: 38 us
  Pallas kernels  36.7 us (96%)
  between operations  1.29 us (3%)
    pallas_call x1, Pallas kernels, cycle(): pl.pallas_call(functools.partial(cycle_kernel, n), out_shape=(pltpu.VMEM(...  35.6 us
    pallas_call x1, Pallas kernels, write_out(): pl.pallas_call(write_kernel, out_shape=(jax.ShapeDtypeStruct(fresh.shape,...  1.07 us

profile of v5, /device:TPU:0, one launch (start us, length us, event | category | flops | bytes accessed | tf_op | source)
XLA Modules:
  0.0 38.0 jit_solution(14678864281103519997)
XLA Ops:
  1.3 35.6 %shard_map.104 = (bf16[4,8,32,512]{3,2,1,0:T(8,128)(2,1)S(1)}, bf16[8,32,512]{2,1,0:T(8,128)(2,1)S(1)}) custom-call(bf16[4,8,32,512]{3,2,1,0:T(8,128)(2,1)} %state_ref.1, s32[1]{0:T(128)S(6)} %copy.11.counts_ref, f32[32,512]{1,0:T(8,128)} %east_ref.1, f32[32,512]{1,0:T(8,128)} %north_ref.1, s32[1,32768]{1,0:T(1,128)} %cells_ref.1, s32[1,32768]{1,0:T(1,128)} %mask_ref.1, ...), custom_call_target="tpu_custom_call" | custom-call | tf_op jit(solution)/shard_map/pallas_call | solution.py:695
  36.9 1.1 %shard_map.105 = (bf16[4,8,32,512]{3,2,1,0:T(8,128)(2,1)}, bf16[8,32,512]{2,1,0:T(8,128)(2,1)}) custom-call(bf16[4,8,32,512]{3,2,1,0:T(8,128)(2,1)S(1)} %get-tuple-element.4.fresh, bf16[8,32,512]{2,1,0:T(8,128)(2,1)S(1)} %get-tuple-element.5.mean), custom_call_target="tpu_custom_call" | custom-call | tf_op jit(solution)/shard_map/pallas_call | solution.py:767

commit v6 on v5

--- a/solution.py
+++ b/solution.py
@@ -359,7 +359,7 @@
         advected[first:last] = whole.reshape(last - first, slots, rows, width)
 
     total = fields * (slots // TOGETHER)
-    early, late = total // 8, 7 * total // 8
+    early = total // 8
     lax.fori_loop(0, slots // TOGETHER, move, 0)
     collect(0, 1)
     lax.fori_loop(slots // TOGETHER, early, move, 0)
@@ -382,12 +382,14 @@
     for d in range(1, SHARERS):
         grid_out(d).start()
 
-    lax.fori_loop(early, late, move, 0)
-
-    def likely(d, carry):
-        source = near_by(SHARERS - d)
-
-        @pl.when(d > 0)
+    lax.fori_loop(early, total, move, 0)
+
+    collect(1, fields)
+
+    def likely(index, carry):
+        source = lax.rem(index + (1 - band) * (SHARERS // 2), SHARERS)
+
+        @pl.when(source != rank)
         def _():
             pltpu.make_async_remote_copy(
                 src_ref=grids.at[source],
@@ -408,10 +410,9 @@
                 )
         return carry
 
-    lax.fori_loop(0, SHARERS, likely, 0)
+    lax.fori_loop(0, SHARERS // 2, likely, 0)
     copy_loglik = to_other(loglik.at[:, edge16, :], loglik_halo, 2)
-    lax.fori_loop(late, total, move, 0)
-    collect(1, fields)
+    lax.fori_loop(SHARERS // 2, SHARERS, likely, 0)
 
     r0 = lax.broadcasted_iota(jnp.int32, (rows, rows), 0)
     r1 = lax.broadcasted_iota(jnp.int32, (rows, rows), 1)
@@ -422,13 +423,10 @@
     dot = functools.partial(
         jnp.dot, precision=lax.Precision.HIGHEST, preferred_element_type=jnp.float32
     )
+    own_part = [dot(own_band, loglik[slot]) for slot in range(slots)]
     copy_loglik.wait()
     smoothed = jnp.concatenate(
-        [
-            dot(own_band, loglik[slot]) + dot(far_band, loglik_halo[slot])
-            for slot in range(slots)
-        ],
-        axis=0,
+        [own_part[slot] + dot(far_band, loglik_halo[slot]) for slot in range(slots)], axis=0
     )
     scores[...] = dot(smoothed, lon_kernel[...]).reshape(slots, rows, width)
 

time: 38.1 us -> 37.8 us (level)
  Pallas kernels: 36.7 us -> 36.3 us
where the time goes in v6:
time: 37.8 us; the launch traced here: 37.6 us
  Pallas kernels  36.3 us (96%)
  between operations  1.29 us (3%)
    pallas_call x1, Pallas kernels, cycle(): pl.pallas_call(functools.partial(cycle_kernel, n), out_shape=(pltpu.VMEM(...  35.3 us
    pallas_call x1, Pallas kernels, write_out(): pl.pallas_call(write_kernel, out_shape=(jax.ShapeDtypeStruct(fresh.shape,...  1.07 us

profile of v6, /device:TPU:0, one launch (start us, length us, event | category | flops | bytes accessed | tf_op | source)
XLA Modules:
  0.0 37.6 jit_solution(17225380918343223029)
XLA Ops:
  1.3 35.3 %shard_map.104 = (bf16[4,8,32,512]{3,2,1,0:T(8,128)(2,1)S(1)}, bf16[8,32,512]{2,1,0:T(8,128)(2,1)S(1)}) custom-call(bf16[4,8,32,512]{3,2,1,0:T(8,128)(2,1)} %state_ref.1, s32[1]{0:T(128)S(6)} %copy.11.counts_ref, f32[32,512]{1,0:T(8,128)} %east_ref.1, f32[32,512]{1,0:T(8,128)} %north_ref.1, s32[1,32768]{1,0:T(1,128)} %cells_ref.1, s32[1,32768]{1,0:T(1,128)} %mask_ref.1, ...), custom_call_target="tpu_custom_call" | custom-call | tf_op jit(solution)/shard_map/pallas_call | solution.py:693
  36.5 1.1 %shard_map.105 = (bf16[4,8,32,512]{3,2,1,0:T(8,128)(2,1)}, bf16[8,32,512]{2,1,0:T(8,128)(2,1)}) custom-call(bf16[4,8,32,512]{3,2,1,0:T(8,128)(2,1)S(1)} %get-tuple-element.4.fresh, bf16[8,32,512]{2,1,0:T(8,128)(2,1)S(1)} %get-tuple-element.5.mean), custom_call_target="tpu_custom_call" | custom-call | tf_op jit(solution)/shard_map/pallas_call | solution.py:765

commit v7 on v6

--- a/solution.py
+++ b/solution.py
@@ -14,7 +14,7 @@
 MESH = pl.DeviceIdType.MESH
 TILE_ROWS = 16
 TILE_COLS = 128
-OBS_BLOCK = 4096
+OBS_BLOCK = 8192
 TOGETHER = 4
 SHARERS = 4
 LEVELS = 32760.0
@@ -40,13 +40,14 @@
     )
     row = cells // width
     column = cells - row * width
-    row_hit = lax.broadcasted_iota(jnp.int32, (rows, count), 0) == row
-    column_hit = jnp.where(
-        lax.broadcasted_iota(jnp.int32, (width, count), 0) == column, 1.0, 0.0
-    ).astype(jnp.bfloat16)
+    short = jnp.int16
+    row_hit = lax.broadcasted_iota(short, (rows, count), 0) == row.astype(short)
+    column_hit = lax.broadcasted_iota(short, (width, count), 0) == column.astype(short)
+    one, none = jnp.ones((), jnp.bfloat16), jnp.zeros((), jnp.bfloat16)
+    column_hit = jnp.where(column_hit, one, none)
     left = jnp.concatenate(
         [
-            jnp.where(row_hit, piece, 0.0).astype(jnp.bfloat16)
+            jnp.where(row_hit, piece.astype(jnp.bfloat16), none)
             for piece in pieces(terms[0]) + pieces(terms[1]) + pieces(terms[2])[:2]
         ],
         axis=0,
@@ -54,6 +55,10 @@
     return lax.dot_general(
         left, column_hit, (((1,), (1,)), ((), ())), preferred_element_type=jnp.float32
     )
+
+
+def cut(values):
+    return [piece.astype(jnp.bfloat16) for piece in pieces(values)]
 
 
 def one_hot(hit):
@@ -183,6 +188,15 @@
     pl.semaphore_signal(barrier, inc=1, device_id={"lat": other}, device_id_type=MESH)
     lax.fori_loop(1, n, greet, 0)
 
+    i0 = lax.broadcasted_iota(jnp.int32, (width, width), 0)
+    i1 = lax.broadcasted_iota(jnp.int32, (width, width), 1)
+    spread_columns[...] = one_hot(i0 == (width // TILE_COLS) * lax.rem(i1, TILE_COLS) + i1 // TILE_COLS)
+    gather_columns[...] = one_hot(i1 == (width // TILE_COLS) * lax.rem(i0, TILE_COLS) + i0 // TILE_COLS)
+    near0 = lax.broadcasted_iota(jnp.int32, (2 * TILE_COLS, TILE_COLS), 0)
+    near1 = lax.broadcasted_iota(jnp.int32, (2 * TILE_COLS, TILE_COLS), 1)
+    for k, piece in enumerate(cut(kernel_values(near0 - TILE_COLS // 2 - near1))):
+        lon_kernel[:, k * TILE_COLS : (k + 1) * TILE_COLS] = piece
+
     for load in loads[5:]:
         load.wait()
     pl.semaphore_wait(barrier, n)
@@ -269,13 +283,6 @@
             device_id={"mem": first_rank + near_by(d)},
             device_id_type=MESH,
         )
-
-    i0 = lax.broadcasted_iota(jnp.int32, (width, width), 0)
-    i1 = lax.broadcasted_iota(jnp.int32, (width, width), 1)
-    spread_columns[...] = one_hot(i0 == across * lax.rem(i1, TILE_COLS) + i1 // TILE_COLS)
-    gather_columns[...] = one_hot(i1 == across * lax.rem(i0, TILE_COLS) + i0 // TILE_COLS)
-    apart = jnp.abs(i0 - i1)
-    lon_kernel[...] = kernel_values(jnp.minimum(apart, width - apart))
 
     near = lax.broadcasted_iota(jnp.int32, (8, width), 0)
     keep = jnp.where(band == 0, near, 7 - near) < STEPS
@@ -428,7 +435,24 @@
     smoothed = jnp.concatenate(
         [own_part[slot] + dot(far_band, loglik_halo[slot]) for slot in range(slots)], axis=0
     )
-    scores[...] = dot(smoothed, lon_kernel[...]).reshape(slots, rows, width)
+    tall = slots * rows
+    smoothed = pltpu.roll(smoothed, TILE_COLS // 2, 1)
+    parts = []
+    for piece in cut(smoothed):
+        around = jnp.concatenate([piece, piece[:, :TILE_COLS]], axis=1)
+        parts += [
+            around[:, c * TILE_COLS : (c + 2) * TILE_COLS] for c in range(across)
+        ]
+    one = permute(jnp.concatenate(parts, axis=0), lon_kernel[:, : 2 * TILE_COLS])
+    three = permute(jnp.concatenate(parts[:across], axis=0), lon_kernel[:, 2 * TILE_COLS :])
+    high, mid, low = (one[k * across * tall : (k + 1) * across * tall] for k in range(3))
+    result = high[:, :TILE_COLS] + (
+        (high[:, TILE_COLS:] + mid[:, :TILE_COLS])
+        + ((mid[:, TILE_COLS:] + low[:, :TILE_COLS]) + three)
+    )
+    for c in range(across):
+        scores[:, :, columns(c)] = result[c * tall : (c + 1) * tall].reshape(slots, rows, TILE_COLS)
+
 
     partner = me + 1 - 2 * lax.rem(me, 2)
     parity = lax.rem(me, 2)
@@ -446,8 +470,8 @@
                 device_id_type=MESH,
             )
             for source, landing, sent_sems, landed_sems in (
+                (send, recv, send_sems, recv_sems),
                 (send_log, recv_log, send_log_sems, recv_log_sems),
-                (send, recv, send_sems, recv_sems),
             )
         ]
 
@@ -543,8 +567,10 @@
 
         return carry
 
-    lax.fori_loop(0, owners // 2, give_pair, 0)
-    lax.fori_loop(0, owners // 2, keep_own, 0)
+    for j in range(middle):
+        give_pair(j, 0)
+    for j in range(middle):
+        keep_own(j, 0)
     lax.fori_loop(0, owners // 2, give_owner, 0)
 
     def back(d):
@@ -601,7 +627,7 @@
             merged[me, plane] = value
 
         def start(d, carry):
-            back(d).start()
+            back(jnp.where(2 * place < middle, half - d, d)).start()
             return carry
 
         lax.fori_loop(1, half, start, 0)
@@ -719,7 +745,7 @@
             pltpu.VMEM((slots, fields, across, rows + 8, TILE_COLS), f32),
             pltpu.VMEM((fields, slots, rows, width), bf16),
             pltpu.VMEM((fields, slots, rows, width), bf16),
-            pltpu.VMEM((width, width), f32),
+            pltpu.VMEM((2 * TILE_COLS, 3 * TILE_COLS), bf16),
             pltpu.VMEM((slots, rows, width), f32),
             pltpu.VMEM((slots, 16, width), f32),
             pltpu.VMEM((slots, rows, width), f32),

time: 37.8 us -> 37.6 us (level)
  no operation moved by 1% of the time
where the time goes in v7:
time: 37.6 us; the launch traced here: 37.5 us
  Pallas kernels  36.2 us (96%)
  between operations  1.29 us (3%)
    pallas_call x1, Pallas kernels, cycle(): pl.pallas_call(functools.partial(cycle_kernel, n), out_shape=(pltpu.VMEM(...  35.1 us
    pallas_call x1, Pallas kernels, write_out(): pl.pallas_call(write_kernel, out_shape=(jax.ShapeDtypeStruct(fresh.shape,...  1.07 us

profile of v7, /device:TPU:0, one launch (start us, length us, event | category | flops | bytes accessed | tf_op | source)
XLA Modules:
  0.0 37.5 jit_solution(1289183536675972681)
XLA Ops:
  1.3 35.1 %shard_map.104 = (bf16[4,8,32,512]{3,2,1,0:T(8,128)(2,1)S(1)}, bf16[8,32,512]{2,1,0:T(8,128)(2,1)S(1)}) custom-call(bf16[4,8,32,512]{3,2,1,0:T(8,128)(2,1)} %state_ref.1, s32[1]{0:T(128)S(6)} %copy.11.counts_ref, f32[32,512]{1,0:T(8,128)} %east_ref.1, f32[32,512]{1,0:T(8,128)} %north_ref.1, s32[1,32768]{1,0:T(1,128)} %cells_ref.1, s32[1,32768]{1,0:T(1,128)} %mask_ref.1, ...), custom_call_target="tpu_custom_call" | custom-call | tf_op jit(solution)/shard_map/pallas_call | solution.py:719
  36.4 1.1 %shard_map.105 = (bf16[4,8,32,512]{3,2,1,0:T(8,128)(2,1)}, bf16[8,32,512]{2,1,0:T(8,128)(2,1)}) custom-call(bf16[4,8,32,512]{3,2,1,0:T(8,128)(2,1)S(1)} %get-tuple-element.4.fresh, bf16[8,32,512]{2,1,0:T(8,128)(2,1)S(1)} %get-tuple-element.5.mean), custom_call_target="tpu_custom_call" | custom-call | tf_op jit(solution)/shard_map/pallas_call | solution.py:791

commit v8 on v6

--- a/solution.py
+++ b/solution.py
@@ -14,7 +14,7 @@
 MESH = pl.DeviceIdType.MESH
 TILE_ROWS = 16
 TILE_COLS = 128
-OBS_BLOCK = 4096
+OBS_BLOCK = 8192
 TOGETHER = 4
 SHARERS = 4
 LEVELS = 32760.0

time: 37.8 us -> 37.5 us (level)
  no operation moved by 1% of the time
where the time goes in v8:
time: 37.5 us; the launch traced here: 37.4 us
  Pallas kernels  36.1 us (96%)
  between operations  1.29 us (3%)
    pallas_call x1, Pallas kernels, cycle(): pl.pallas_call(functools.partial(cycle_kernel, n), out_shape=(pltpu.VMEM(...  35 us
    pallas_call x1, Pallas kernels, write_out(): pl.pallas_call(write_kernel, out_shape=(jax.ShapeDtypeStruct(fresh.shape,...  1.07 us

profile of v8, /device:TPU:0, one launch (start us, length us, event | category | flops | bytes accessed | tf_op | source)
XLA Modules:
  0.0 37.4 jit_solution(15654549970918658520)
XLA Ops:
  1.3 35.0 %shard_map.104 = (bf16[4,8,32,512]{3,2,1,0:T(8,128)(2,1)S(1)}, bf16[8,32,512]{2,1,0:T(8,128)(2,1)S(1)}) custom-call(bf16[4,8,32,512]{3,2,1,0:T(8,128)(2,1)} %state_ref.1, s32[1]{0:T(128)S(6)} %copy.11.counts_ref, f32[32,512]{1,0:T(8,128)} %east_ref.1, f32[32,512]{1,0:T(8,128)} %north_ref.1, s32[1,32768]{1,0:T(1,128)} %cells_ref.1, s32[1,32768]{1,0:T(1,128)} %mask_ref.1, ...), custom_call_target="tpu_custom_call" | custom-call | tf_op jit(solution)/shard_map/pallas_call | solution.py:693
  36.3 1.1 %shard_map.105 = (bf16[4,8,32,512]{3,2,1,0:T(8,128)(2,1)}, bf16[8,32,512]{2,1,0:T(8,128)(2,1)}) custom-call(bf16[4,8,32,512]{3,2,1,0:T(8,128)(2,1)S(1)} %get-tuple-element.4.fresh, bf16[8,32,512]{2,1,0:T(8,128)(2,1)S(1)} %get-tuple-element.5.mean), custom_call_target="tpu_custom_call" | custom-call | tf_op jit(solution)/shard_map/pallas_call | solution.py:765
